TPU v7x, 512 devices: a whole 4x4x16 slice. The times are simulated.
512 devices in a mesh: tm: 8 (over z_hi, core), tile: 16 (over x, y), head: 4 (over z_lo).
Axes of the slice: x: 4, y: 4, z: 16 (z_hi: 4, z_lo: 4; z = z_hi * 4 + z_lo), core: 2. Of those that a mesh axis runs over, the one named last changes fastest.
Arguments:
- query: bfloat16 [8, 16, 2, 16, 16, 1536], P('tm', 'tile', None, None, None, 'head'), may hold values from -80 to 80
- keys: bfloat16 [8, 16, 2, 16, 16, 1536], P('tm', 'tile', None, None, None, 'head'), may hold values from -80 to 80
- values: bfloat16 [8, 16, 2, 16, 16, 1536], P('tm', 'tile', None, None, None, 'head'), may hold values from -6 to 6
- out_weight: bfloat16 [1536, 1536], P('head'), may hold values from -0.15625 to 0.15625
- radius: int32 [12], P('head'), may hold values from 1 to 4
- block_mask: int32 [12, 8, 8], P('head'), may hold values from 0 to 1, as said below
Outputs:
- mixed: bfloat16 [8, 16, 512, 1536], P('tm', 'tile', 'head')
Inputs may be any that keep to these rules, and one draw needn't show every extreme that they name: For every head, block_mask is 1 on the diagonal of its table and 0 above it.
All inputs are finite; a program needn't handle non-finite values.
Results may differ from a plain program's by a relative error of at most 0.015.
Values may be sent and summed in bfloat16 or wider, within the bound.
A program may use at most 128 MiB of HBM per device.

v0:
```python
import math

import jax
import jax.numpy as jnp
from jax import lax
from jax.sharding import PartitionSpec as P

RMAX = 4


def passed_along(value, axis, by):
    peers = lax.axis_size(axis)
    pairs = [(i, i + by) for i in range(peers) if 0 <= i + by < peers]
    return lax.ppermute(value, axis, pairs)


def widen(key_part, value_part, span, row_move, col_move):
    grid = math.isqrt(lax.axis_size("tile"))
    above = None
    below = None
    for offset in (grid, -grid):
        if offset > 0:
            face_key = key_part[:, :, key_part.shape[2] - span :]
            face_value = value_part[:, :, value_part.shape[2] - span :]
        else:
            face_key = key_part[:, :, :span]
            face_value = value_part[:, :, :span]
        got = row_move(face_key, face_value, offset)
        if offset > 0:
            above = got
        else:
            below = got
    key_rows = jnp.concatenate([above[0], key_part, below[0]], axis=2)
    value_rows = jnp.concatenate([above[1], value_part, below[1]], axis=2)
    left = None
    right = None
    for offset in (1, -1):
        if offset > 0:
            face_key = key_rows[:, :, :, key_rows.shape[3] - span :]
            face_value = value_rows[:, :, :, value_rows.shape[3] - span :]
        else:
            face_key = key_rows[:, :, :, :span]
            face_value = value_rows[:, :, :, :span]
        got = col_move(face_key, face_value, offset)
        if offset > 0:
            left = got
        else:
            right = got
    key_full = jnp.concatenate([left[0], key_rows, right[0]], axis=3)
    value_full = jnp.concatenate([left[1], value_rows, right[1]], axis=3)
    return (key_full, value_full)


def windows_of(block, half_high, half_wide, win_high, win_wide, heads_here, head_dim):
    parts = []
    for band in (0, 1):
        for strip in (0, 1):
            parts.append(
                block[
                    :,
                    band * half_high : band * half_high + win_high,
                    strip * half_wide : strip * half_wide + win_wide,
                ]
            )
    stacked = jnp.stack(parts)
    return stacked.reshape(4, -1, heads_here, head_dim)


def per_device(query, keys, values, out_weight, radius, block_mask):
    span = RMAX
    grid = math.isqrt(lax.axis_size("tile"))
    tile_at = lax.axis_index("tile")
    row_at = tile_at // grid
    col_at = tile_at % grid
    stretch_at = lax.axis_index("tm")
    frames, high, wide, channels = query.shape[2:]
    heads_here = radius.shape[0]
    head_dim = channels // heads_here
    tokens_here = frames * high * wide
    half_high = high // 2
    half_wide = wide // 2
    win_high = half_high + 2 * span
    win_wide = half_wide + 2 * span
    quarter = frames * half_high * half_wide
    queries = query[0, 0].reshape(frames, 2, half_high, 2, half_wide, channels)
    queries = queries.transpose(1, 3, 0, 2, 4, 5).reshape(4, quarter, heads_here, head_dim)
    query_y = jnp.broadcast_to(
        jnp.arange(half_high, dtype=jnp.int32)[None, :, None], (frames, half_high, half_wide)
    ).reshape(-1)
    query_x = jnp.broadcast_to(
        jnp.arange(half_wide, dtype=jnp.int32)[None, None, :], (frames, half_high, half_wide)
    ).reshape(-1)
    key_y = jnp.broadcast_to(
        jnp.arange(win_high, dtype=jnp.int32)[None, :, None] - span, (frames, win_high, win_wide)
    ).reshape(-1)
    key_x = jnp.broadcast_to(
        jnp.arange(win_wide, dtype=jnp.int32)[None, None, :] - span, (frames, win_high, win_wide)
    ).reshape(-1)
    band_at = jnp.array([0, 0, 1, 1], dtype=jnp.int32)
    strip_at = jnp.array([0, 1, 0, 1], dtype=jnp.int32)
    global_y = row_at * high + band_at[:, None] * half_high + key_y[None, :]
    global_x = col_at * wide + strip_at[:, None] * half_wide + key_x[None, :]
    inside = (global_y >= 0) & (global_y < grid * high) & (global_x >= 0) & (global_x < grid * wide)
    distance = jnp.maximum(
        jnp.abs(query_y[:, None] - key_y[None, :]), jnp.abs(query_x[:, None] - key_x[None, :])
    )
    near = distance[None, :, :] <= radius[:, None, None]
    allowed = near[None, :, :, :] & inside[:, None, None, :]
    scale = 1.0 / math.sqrt(head_dim)
    initial = (
        jnp.full((4, heads_here, quarter), -1e30, jnp.float32),
        jnp.zeros((4, heads_here, quarter), jnp.float32),
        jnp.zeros((4, heads_here, quarter, head_dim), jnp.float32),
    )

    def all_row_move(face_key, face_value, offset):
        return passed_along((face_key, face_value), "tile", offset)

    def all_col_move(face_key, face_value, offset):
        return passed_along((face_key, face_value), "tile", offset)

    key_all, value_all = (
        lax.all_gather(keys[0], "tm", axis=0, tiled=True),
        lax.all_gather(values[0], "tm", axis=0, tiled=True),
    )
    key_full, value_full = widen(key_all, value_all, span, all_row_move, all_col_move)
    piece = (key_full, value_full)
    count = piece[0].shape[0]
    stretch_ids = jnp.arange(count, dtype=jnp.int32)

    def one_stretch(state, item):
        key_block, value_block, stretch_id = item
        visible = (
            lax.dynamic_slice_in_dim(
                lax.dynamic_index_in_dim(block_mask, stretch_at, 1, False), stretch_id, 1, 1
            )[:, 0]
            > 0
        )
        best, total, acc = state
        key_win = windows_of(
            key_block, half_high, half_wide, win_high, win_wide, heads_here, head_dim
        )
        value_win = windows_of(
            value_block, half_high, half_wide, win_high, win_wide, heads_here, head_dim
        )
        usable = allowed & visible[None, :, None, None]
        scores = (
            jnp.einsum("nqhd,nkhd->nhqk", queries, key_win, preferred_element_type=jnp.float32)
            * scale
        )
        masked = jnp.where(usable, scores, jnp.float32(-1e30))
        fresh = jnp.maximum(best, jnp.max(masked, axis=3))
        probs = jnp.where(usable, jnp.exp(scores - fresh[..., None]), jnp.float32(0.0))
        shrink = jnp.exp(best - fresh)
        total = total * shrink + jnp.sum(probs, axis=3)
        acc = acc * shrink[..., None] + jnp.einsum(
            "nhqk,nkhd->nhqd",
            probs.astype(jnp.bfloat16),
            value_win,
            preferred_element_type=jnp.float32,
        )
        result = (fresh, total, acc)
        return (result, None)

    final, unused = lax.scan(one_stretch, initial, (piece[0], piece[1], stretch_ids))
    best, total, acc = final
    attn = (acc / total[..., None]).astype(jnp.bfloat16)
    attn = attn.transpose(0, 2, 1, 3).reshape(
        2, 2, frames, half_high, half_wide, heads_here * head_dim
    )
    attn = attn.transpose(2, 0, 3, 1, 4, 5).reshape(tokens_here, heads_here * head_dim)
    mixed = lax.psum_scatter(
        jnp.dot(attn, out_weight, preferred_element_type=jnp.float32).astype(jnp.bfloat16),
        "head",
        scatter_dimension=0,
        tiled=True,
    )
    return mixed.reshape(1, 1, -1, out_weight.shape[1])


def solution(mesh):
    in_specs = (
        P("tm", "tile", None, None, None, "head"),
        P("tm", "tile", None, None, None, "head"),
        P("tm", "tile", None, None, None, "head"),
        P("head", None),
        P("head"),
        P("head", None, None),
    )
    out_specs = P("tm", "tile", "head", None)
    return jax.shard_map(
        per_device, mesh=mesh, in_specs=in_specs, out_specs=out_specs, check_vma=False
    )
```

profile of v0, /device:TPU:1, one launch (start us, length us, event | category | flops | bytes accessed | tf_op | source)
XLA Modules:
  0.0 517.4 jit_solution(15858110646869679896)
XLA Ops:
  8.1 85.1 %all-gather.7.cloned.1.call-done = bf16[8,1,2,16,16,384]{5,4,3,2,1,0:T(8,128)(2,1)} async-done(((bf16[1,1,2,16,16,384]{5,4,3,2,1,0:T(8,128)(2,1)}), bf16[8,1,2,16,16,384]{5,4,3,2,1,0:T(8,128)(2,1)}) %all-gather.7.cloned.1.call-update) | async-done | bytes 3145744 | tf_op jit(solution)/shard_map/all_gather | solution.py:124
  93.2 2.5 fusion.46
  95.7 3.8 collective-permute-start.4
  102.1 14.4 %collective-permute-done.4 = bf16[8,2,4,16,384]{4,3,2,1,0:T(8,128)(2,1)S(1)} collective-permute-done((bf16[8,2,4,16,384]{4,3,2,1,0:T(8,128)(2,1)}, bf16[8,2,4,16,384]{4,3,2,1,0:T(8,128)(2,1)S(1)}, u32[]{:S(2)}, u32[]{:S(2)}) %collective-permute-start.4) | collective-permute-done | bytes 786464 | tf_op jit(solution)/shard_map/ppermute | solution.py:14
  116.5 3.6 collective-permute-done.5
  120.1 3.5 pad_maximum_fusion.4
  123.6 4.2 collective-permute-start.6
  129.0 40.4 %all-gather.5.cloned.1.call-done = bf16[8,1,2,16,16,384]{5,4,3,2,1,0:T(8,128)(2,1)} async-done(((bf16[1,1,2,16,16,384]{5,4,3,2,1,0:T(8,128)(2,1)}), bf16[8,1,2,16,16,384]{5,4,3,2,1,0:T(8,128)(2,1)}) %all-gather.5.cloned.1.call-update) | async-done | bytes 3145744 | tf_op jit(solution)/shard_map/all_gather | solution.py:123
  169.5 2.8 fusion.47
  172.2 3.8 collective-permute-start
  186.3 1.8 copy.45
  188.1 2.1 reshape.220
  190.2 1.9 copy.40
  192.0 1.4 copy.39
  195.7 1.5 broadcast_compare_fusion
  197.2 2.9 pad_maximum_fusion.7
  200.1 3.2 collective-permute-start.2
  203.3 1.7 collective-permute-start.3
  205.1 7.7 %pad_maximum_fusion.1 = bf16[8,2,24,24,384]{4,3,2,1,0:T(8,128)(2,1)} fusion(bf16[8,2,24,4,384]{4,3,2,1,0:T(4,128)(2,1)} %collective-permute-done.7, bf16[8,2,4,16,384]{4,3,2,1,0:T(8,128)(2,1)S(1)} %collective-permute-done.5, bf16[8,2,16,16,384]{4,3,2,1,0:T(8,128)(2,1)S(1)} %bitcast.74, bf16[8,2,4,16,384]{4,3,2,1,0:T(8,128)(2,1)S(1)} %collective-permute-done.4, ...), kind=kLoop, calls=%fused_computation.46 | loop fusion | flops 35389440 | bytes 14155776 | tf_op jit(solution)/shard_map/concatenate | solution.py:50
  212.8 14.5 %collective-permute-done.2 = bf16[8,2,24,4,384]{4,3,2,1,0:T(4,128)(2,1)S(1)} collective-permute-done((bf16[8,2,24,4,384]{4,3,2,1,0:T(4,128)(2,1)S(1)}, bf16[8,2,24,4,384]{4,3,2,1,0:T(4,128)(2,1)S(1)}, u32[]{:S(2)}, u32[]{:S(2)}) %collective-permute-start.2) | collective-permute-done | bytes 1179680 | tf_op jit(solution)/shard_map/ppermute | solution.py:14
  227.4 4.2 collective-permute-done.3
  231.5 7.6 %pad_maximum_fusion = bf16[8,2,24,24,384]{4,3,2,1,0:T(8,128)(2,1)} fusion(bf16[8,2,24,4,384]{4,3,2,1,0:T(4,128)(2,1)S(1)} %collective-permute-done.3, bf16[8,2,4,16,384]{4,3,2,1,0:T(8,128)(2,1)} %collective-permute-done.1, bf16[8,2,16,16,384]{4,3,2,1,0:T(8,128)(2,1)S(1)} %bitcast.71, bf16[8,2,4,16,384]{4,3,2,1,0:T(8,128)(2,1)S(1)} %collective-permute-done, ...), kind=kLoop, calls=%fused_computation.45 | loop fusion | flops 35389440 | bytes 14155776 | tf_op jit(solution)/shard_map/concatenate | solution.py:49
  239.1 221.7 %while.18 = (s32[]{:T(128)}, f32[4,3,128]{2,1,0:T(4,128)S(1)}, f32[4,3,128]{2,1,0:T(4,128)S(1)}, f32[4,3,128,128]{3,2,1,0:T(8,128)}, s32[8]{0:T(128)S(1)}, /*ind...) while((s32[]{:T(128)}, f32[4,3,128]{2,1,0:T(4,128)S(1)}, ...), condition=%wide.region_3.4_spmd.clone, body=%wide.region_0.3_spmd.clone.sunk | while | flops 421338624 | bytes 41597296 | solution.py:165
  242.2 1.6 dynamic-slice_bitcast_fusion.3
  244.9 1.4 stack.48
  250.4 4.0 fusion.64
  254.4 2.4 fusion.65
  262.2 4.4 fusion.68
  269.7 1.6 dynamic-slice_bitcast_fusion.3
  272.4 1.4 stack.48
  277.9 4.0 fusion.64
  281.9 2.4 fusion.65
  289.7 4.7 fusion.68
  297.5 1.6 dynamic-slice_bitcast_fusion.3
  300.1 1.4 stack.48
  305.7 4.0 fusion.64
  309.7 2.4 fusion.65
  317.4 4.7 fusion.68
  325.2 1.6 dynamic-slice_bitcast_fusion.3
  327.9 1.4 stack.48
  333.4 4.0 fusion.64
  337.4 2.4 fusion.65
  345.2 4.7 fusion.68
  353.0 1.6 dynamic-slice_bitcast_fusion.3
  361.2 4.0 fusion.64
  365.2 2.4 fusion.65
  372.9 4.7 fusion.68
  380.7 1.6 dynamic-slice_bitcast_fusion.3
  383.4 1.4 stack.48
  388.9 4.0 fusion.64
  392.9 2.4 fusion.65
  400.7 4.7 fusion.68
  408.5 1.6 dynamic-slice_bitcast_fusion.3
  411.1 1.4 stack.48
  416.6 4.0 fusion.64
  420.7 2.4 fusion.65
  428.4 4.7 fusion.68
  436.2 1.6 dynamic-slice_bitcast_fusion.3
  444.4 4.0 fusion.64
  448.4 2.4 fusion.65
  456.1 4.7 fusion.68
  460.8 1.4 fusion.40
  463.0 2.2 convolution_convert_fusion
  465.2 45.7 %reduce-scatter.2.cloned.1.call-done = bf16[128,1536]{1,0:T(8,128)(2,1)} async-done(((bf16[512,1536]{1,0:T(8,128)(2,1)}), bf16[128,1536]{1,0:T(8,128)(2,1)}) %reduce-scatter.2.cloned.1.call-update) | async-done | bytes 393232 | tf_op jit(solution)/shard_map/reduce_scatter | solution.py:172
  (282 shorter events, 114.4 us)
Async XLA Ops:
  6.5 456.4 %copy-start = (bf16[384,1536]{1,0:T(8,128)(2,1)S(1)}, bf16[384,1536]{1,0:T(8,128)(2,1)}, u32[]{:S(2)}) copy-start(bf16[384,1536]{1,0:T(8,128)(2,1)} %param.13) | copy-start | bytes 3538948
  6.5 86.7 %all-gather.7.cloned.1.call-start = ((), (), s32[]{:S(2)}) async-start(), calls=%async_computation.3 | async-start | bytes 3538944 | tf_op jit(solution)/shard_map/all_gather | solution.py:124
  7.3 162.2 %all-gather.5.cloned.1.call-start = ((), (), s32[]{:S(2)}) async-start(), calls=%async_computation.2 | async-start | bytes 3538944 | tf_op jit(solution)/shard_map/all_gather | solution.py:123
  8.0 502.9 %reduce-scatter.2.cloned.1.call-start = ((), (), s32[]{:S(2)}) async-start(), calls=%async_computation.1 | async-start | bytes 1966080 | tf_op jit(solution)/shard_map/reduce_scatter | solution.py:172
  95.7 20.8 %collective-permute-start.4 = (bf16[8,2,4,16,384]{4,3,2,1,0:T(8,128)(2,1)}, bf16[8,2,4,16,384]{4,3,2,1,0:T(8,128)(2,1)S(1)}, u32[]{:S(2)}, u32[]{:S(2)}) collective-permute-start(bf16[8,2,4,16,384]{4,3,2,1,0:T(8,128)(2,1)} %get-tuple-element.310), channel_id=1, source_target_pairs={{0,16},{4,20},{8,24},{12,28},{16,32},{20,36},{24,40},{28,44},{32,4... | collective-permute-start | bytes 2359304 | tf_op jit(solution)/shard_map/ppermute | solution.py:14
  99.5 20.6 %collective-permute-start.5 = (bf16[8,2,4,16,384]{4,3,2,1,0:T(8,128)(2,1)S(1)}, bf16[8,2,4,16,384]{4,3,2,1,0:T(8,128)(2,1)S(1)}, u32[]{:S(2)}, u32[]{:S(2)}) collective-permute-start(bf16[8,2,4,16,384]{4,3,2,1,0:T(8,128)(2,1)S(1)} %get-tuple-element.311), channel_id=1, source_target_pairs={{16,0},{20,4},{24,8},{28,12},{32,16},{36,20},{40,24},{44,28},{48,3... | collective-permute-start | bytes 2359304 | tf_op jit(solution)/shard_map/ppermute | solution.py:14
  123.6 81.5 %collective-permute-start.6 = (bf16[8,2,24,4,384]{4,3,2,1,0:T(4,128)(2,1)}, bf16[8,2,24,4,384]{4,3,2,1,0:T(4,128)(2,1)}, u32[]{:S(2)}, u32[]{:S(2)}) collective-permute-start(bf16[8,2,24,4,384]{4,3,2,1,0:T(4,128)(2,1)} %get-tuple-element.306), channel_id=1, source_target_pairs={{0,4},{4,8},{8,12},{12,16},{16,20},{20,24},{24,28},{28,32},{32,36}... | collective-permute-start | bytes 3538952 | tf_op jit(solution)/shard_map/ppermute | solution.py:14
  127.8 77.3 %collective-permute-start.7 = (bf16[8,2,24,4,384]{4,3,2,1,0:T(4,128)(2,1)}, bf16[8,2,24,4,384]{4,3,2,1,0:T(4,128)(2,1)}, u32[]{:S(2)}, u32[]{:S(2)}) collective-permute-start(bf16[8,2,24,4,384]{4,3,2,1,0:T(4,128)(2,1)} %get-tuple-element.307), channel_id=1, source_target_pairs={{4,0},{8,4},{12,8},{16,12},{20,16},{24,20},{28,24},{32,28},{36,32}... | collective-permute-start | bytes 3538952 | tf_op jit(solution)/shard_map/ppermute | solution.py:14
  172.2 24.9 %collective-permute-start = (bf16[8,2,4,16,384]{4,3,2,1,0:T(8,128)(2,1)}, bf16[8,2,4,16,384]{4,3,2,1,0:T(8,128)(2,1)S(1)}, u32[]{:S(2)}, u32[]{:S(2)}) collective-permute-start(bf16[8,2,4,16,384]{4,3,2,1,0:T(8,128)(2,1)} %get-tuple-element.312), channel_id=1, source_target_pairs={{0,16},{4,20},{8,24},{12,28},{16,32},{20,36},{24,40},{28,44},{32,4... | collective-permute-start | bytes 2359304 | tf_op jit(solution)/shard_map/ppermute | solution.py:14
  176.1 21.1 %collective-permute-start.1 = (bf16[8,2,4,16,384]{4,3,2,1,0:T(8,128)(2,1)}, bf16[8,2,4,16,384]{4,3,2,1,0:T(8,128)(2,1)}, u32[]{:S(2)}, u32[]{:S(2)}) collective-permute-start(bf16[8,2,4,16,384]{4,3,2,1,0:T(8,128)(2,1)} %get-tuple-element.313), channel_id=1, source_target_pairs={{16,0},{20,4},{24,8},{28,12},{32,16},{36,20},{40,24},{44,28},{48,3... | collective-permute-start | bytes 2359304 | tf_op jit(solution)/shard_map/ppermute | solution.py:14
  177.4 0.5 copy-start.7
  197.2 7.9 %copy-start.2 = (bf16[8,1,2,16,16,384]{5,4,3,2,1,0:T(8,128)(2,1)S(1)}, bf16[8,1,2,16,16,384]{5,4,3,2,1,0:T(8,128)(2,1)}, u32[]{:S(2)}) copy-start(bf16[8,1,2,16,16,384]{5,4,3,2,1,0:T(8,128)(2,1)} %all-gather.7.cloned.1.call-done) | copy-start | bytes 9437188
  200.1 27.2 %collective-permute-start.2 = (bf16[8,2,24,4,384]{4,3,2,1,0:T(4,128)(2,1)S(1)}, bf16[8,2,24,4,384]{4,3,2,1,0:T(4,128)(2,1)S(1)}, u32[]{:S(2)}, u32[]{:S(2)}) collective-permute-start(bf16[8,2,24,4,384]{4,3,2,1,0:T(4,128)(2,1)S(1)} %get-tuple-element.308), channel_id=1, source_target_pairs={{0,4},{4,8},{8,12},{12,16},{16,20},{20,24},{24,28},{28,32},{32,36}... | collective-permute-start | bytes 3538952 | tf_op jit(solution)/shard_map/ppermute | solution.py:14
  203.3 28.2 %copy-start.1 = (bf16[8,1,2,16,16,384]{5,4,3,2,1,0:T(8,128)(2,1)S(1)}, bf16[8,1,2,16,16,384]{5,4,3,2,1,0:T(8,128)(2,1)}, u32[]{:S(2)}) copy-start(bf16[8,1,2,16,16,384]{5,4,3,2,1,0:T(8,128)(2,1)} %all-gather.5.cloned.1.call-done) | copy-start | bytes 9437188
  203.3 28.2 %collective-permute-start.3 = (bf16[8,2,24,4,384]{4,3,2,1,0:T(4,128)(2,1)S(1)}, bf16[8,2,24,4,384]{4,3,2,1,0:T(4,128)(2,1)S(1)}, u32[]{:S(2)}, u32[]{:S(2)}) collective-permute-start(bf16[8,2,24,4,384]{4,3,2,1,0:T(4,128)(2,1)S(1)} %get-tuple-element.309), channel_id=1, source_target_pairs={{4,0},{8,4},{12,8},{16,12},{20,16},{24,20},{28,24},{32,28},{36,32}... | collective-permute-start | bytes 3538952 | tf_op jit(solution)/shard_map/ppermute | solution.py:14
  248.5 1.9 copy-start.6
  250.4 4.0 copy-start.5
  260.1 1.9 copy-start.3
  261.1 1.1 copy-start.4
  276.0 1.9 copy-start.6
  277.9 4.0 copy-start.5
  287.6 1.9 copy-start.3
  288.6 1.1 copy-start.4
  303.7 1.9 copy-start.6
  305.7 4.0 copy-start.5
  315.4 1.9 copy-start.3
  316.3 1.1 copy-start.4
  331.5 1.9 copy-start.6
  333.4 4.0 copy-start.5
  343.1 1.9 copy-start.3
  344.1 1.1 copy-start.4
  359.2 1.9 copy-start.6
  361.1 4.0 copy-start.5
  370.9 1.9 copy-start.3
  371.8 1.1 copy-start.4
  387.0 1.9 copy-start.6
  388.9 4.0 copy-start.5
  398.6 1.9 copy-start.3
  399.6 1.1 copy-start.4
  414.7 1.9 copy-start.6
  416.6 4.0 copy-start.5
  426.4 1.9 copy-start.3
  427.3 1.1 copy-start.4
  442.5 1.9 copy-start.6
  444.4 4.0 copy-start.5
  454.1 1.9 copy-start.3
  455.1 1.1 copy-start.4
Sparse Core Ops, SparseCore 0:
  9.5 83.6 all-gather.6
  95.3 74.1 all-gather.4
  465.3 45.5 reduce-scatter.1
where the time goes:
time: 520 us; the launch traced here: 517 us
  waiting for transfers between devices  209 us (40%)
  local copies, waits for them, and re-layouts  134 us (26%)
  matrix products  71.3 us (14%)
  other arithmetic  53.4 us (10%)
  starting transfers between devices  20.7 us (4%)
  loops' own time  15.8 us (3%)
  between operations  13.3 us (3%)
    all_gather x1, waiting for transfers between devices, per_device(): lax.all_gather(values[0], 'tm', axis=0, tiled=True)  85.1 us
    another operation x128, local copies, waits for them, and re-layouts, windows_of(): stacked = jnp.stack(parts)  77.2 us
    reduce_scatter x1, waiting for transfers between devices, per_device(): lax.psum_scatter(jnp.dot(attn, out_weight, preferred_element_type=jnp.flo...  45.7 us
    all_gather x1, waiting for transfers between devices, per_device(): lax.all_gather(keys[0], 'tm', axis=0, tiled=True)  40.4 us
    dot_general x8, matrix products, one_stretch(): jnp.einsum('nhqk,nkhd->nhqd', probs.astype(jnp.bfloat16), value_win, pref...  37.1 us
    ppermute x8, waiting for transfers between devices, passed_along(): return lax.ppermute(value, axis, pairs)  36.7 us
    dot_general x8, matrix products, one_stretch(): jnp.einsum('nqhd,nkhd->nhqk', queries, key_win, preferred_element_type=jn...  32 us
    ppermute x8, starting transfers between devices, passed_along(): return lax.ppermute(value, axis, pairs)  20.6 us
  transfers between devices with their start and end apart: 11, of which 7 were waited for; matrix products, arithmetic and copies ran while one was open for 8% of the time, Pallas kernels for 0%

commit v1 on v0

v1 whole, which is shorter than its diff:
```python
import functools
import math

import jax
import jax.numpy as jnp
from jax import lax
from jax.experimental import pallas as pl
from jax.experimental.pallas import tpu as pltpu
from jax.sharding import PartitionSpec as P

MESH = pl.DeviceIdType.MESH
LOW = -1e30
STEPS = 6
ROWS = 272
LAG_UP = 1
LAG_END = 2


def attend(scale, q_ref, k_ref, v_ref, radius_ref, mask_ref, out_ref, *scratch):
    (kv, qb, pb, rb, ub, gb, ab, ar, bias, halo_s, halo_r, down_s, down_r, pair_s, pair_r,
     part_s, part_r, up_s, up_r, swap_s, swap_r) = scratch
    tm = lax.axis_index("tm")
    tile = lax.axis_index("tile")
    head = lax.axis_index("head")
    n_tm = lax.axis_size("tm")
    n_head = lax.axis_size("head")
    grid = math.isqrt(lax.axis_size("tile"))
    chips = n_tm // 2
    chip, core = tm // 2, tm % 2
    other = 1 - core
    row, col = tile // grid, tile % grid
    sibling = {"tm": chip * 2 + other}
    lower = {"tm": (tm + n_tm - 2) % n_tm}
    upper = {"tm": (tm + 2) % n_tm}

    def remote(src, dst, send, recv, device):
        return pltpu.make_async_remote_copy(
            src_ref=src, dst_ref=dst, send_sem=send, recv_sem=recv, device_id=device, device_id_type=MESH
        )

    sides = [(dy, dx) for dy in (-1, 0, 1) for dx in (-1, 0, 1) if (dy, dx) != (0, 0)]

    def on_grid(dy, dx):
        return (row + dy >= 0) & (row + dy < grid) & (col + dx >= 0) & (col + dx < grid)

    barrier = pltpu.get_barrier_semaphore()
    count = jnp.int32(2 + n_head)
    for device in (sibling, lower, upper):
        pl.semaphore_signal(barrier, inc=1, device_id=device, device_id_type=MESH)
    for off in range(1, n_head):
        pl.semaphore_signal(barrier, inc=1, device_id={"head": (head + off) % n_head}, device_id_type=MESH)
    for dy, dx in sides:
        count = count + on_grid(dy, dx).astype(jnp.int32)

        @pl.when(on_grid(dy, dx))
        def _():
            pl.semaphore_signal(barrier, inc=1, device_id={"tile": tile + dy * grid + dx}, device_id_type=MESH)

    for frame in (0, 1):
        for band in (0, 1):
            for pair in range(4):
                rows = q_ref[pl.ds(frame * 256 + (band * 8 + pair * 2) * 16, 32), :].astype(jnp.float32)
                for strip in (0, 1):
                    both = jnp.concatenate([rows[8 * strip : 8 * strip + 8], rows[16 + 8 * strip : 24 + 8 * strip]], axis=0)
                    both = both.astype(jnp.bfloat16)
                    for t in range(3):
                        qb[0, core, 2 * t + band, strip, pl.ds(frame * 64 + pair * 16, 16), :] = both[:, 128 * t : 128 * t + 128]

    top = lax.broadcasted_iota(jnp.int32, (8, 384), 0) < 4
    for which, ref in ((0, k_ref), (1, v_ref)):
        for frame in (0, 1):
            for by in range(4):
                rows = ref[pl.ds(frame * 256 + by * 64, 64), :].astype(jnp.float32)
                for bx in range(4):
                    start = 8 * (bx // 2)
                    halves = []
                    for y in (0, 2):
                        first = rows[16 * y + start : 16 * y + start + 8]
                        second = rows[16 * y + 16 + start : 16 * y + 24 + start]
                        if bx % 2 == 0:
                            halves.append(jnp.where(top, first, pltpu.roll(second, 4, 0)))
                        else:
                            halves.append(jnp.where(top, pltpu.roll(first, 4, 0), second))
                    block = jnp.concatenate(halves, axis=0).astype(jnp.bfloat16)
                    for t in range(3):
                        kv[which, t, 1 + by, 1 + bx, pl.ds(frame * 16, 16), :] = block[:, 128 * t : 128 * t + 128]

    pl.semaphore_wait(barrier, count)

    def down(kind, step):
        src, dst = ((0, 1), (1, 2), (0, 3))[kind]
        return remote(
            qb.at[src, core, step], qb.at[dst, core, step], down_s.at[kind, step], down_r.at[kind, step],
            upper if kind == 2 else lower,
        )

    def pair_of(d, step, slot):
        return remote(qb.at[d, slot, step], qb.at[d, slot, step], pair_s.at[d, step], pair_r.at[d, step], sibling)

    def part_of(d, step):
        return remote(pb.at[d, other, step], rb.at[d, step], part_s.at[d, step], part_r.at[d, step], sibling)

    def up(d, step):
        e = {2: 0, 1: 1, 3: 2}[d]
        return remote(
            ub.at[d - 1, step], gb.at[e, step], up_s.at[e, step], up_r.at[e, step], lower if d == 3 else upper
        )

    def halo(number):
        dy, dx = sides[number]
        src = {-1: slice(1, 2), 0: slice(1, 5), 1: slice(4, 5)}
        dst = {-1: slice(5, 6), 0: slice(1, 5), 1: slice(0, 1)}
        return remote(
            kv.at[:, :, src[dy], src[dx]], kv.at[:, :, dst[dy], dst[dx]], halo_s.at[number], halo_r.at[number],
            {"tile": (tile + dy * grid + dx) % (grid * grid)},
        )

    def swap(step, frame):
        return remote(
            ab.at[step, frame], ar.at[head, step // 2], swap_s.at[step, frame], swap_r.at[head, step // 2],
            {"head": frame * 2 + step % 2},
        )

    @pl.loop(0, STEPS)
    def _(step):
        @pl.when(chip >= 1)
        def _():
            down(0, step).start()

        @pl.when(chip == chips - 1)
        def _():
            down(2, step).start()

        @pl.when(core == 1)
        def _():
            pair_of(0, step, core).start()

    for number, (dy, dx) in enumerate(sides):
        @pl.when(on_grid(dy, dx))
        def _():
            halo(number).start()

    none = jnp.zeros((2, 3, 1, 6, 32, 128), jnp.bfloat16)
    for edge, at in ((row == 0, 0), (row == grid - 1, 5)):
        @pl.when(edge)
        def _():
            kv[:, :, at : at + 1, :] = none
    for edge, at in ((col == 0, 0), (col == grid - 1, 5)):
        @pl.when(edge)
        def _():
            kv[:, :, :, at : at + 1] = none.reshape(2, 3, 6, 1, 32, 128)

    def without(ref):
        @pl.loop(0, STEPS)
        def _(step):
            ref[step] = jnp.concatenate([jnp.zeros((256, 128), jnp.float32), jnp.full((16, 128), LOW, jnp.float32)], axis=0).astype(jnp.bfloat16)

    @pl.when(chip == 0)
    def _():
        without(gb.at[0])
        without(gb.at[1])

    @pl.when(chip != chips - 1)
    def _():
        without(gb.at[2])

    @pl.when(core == 0)
    def _():
        without(rb.at[0])

    query_at = lax.broadcasted_iota(jnp.int32, (128, 512), 0)
    key_at = lax.broadcasted_iota(jnp.int32, (128, 512), 1)
    query_y, query_x = (query_at >> 3) & 7, query_at & 7
    key_y = ((key_at >> 7) & 3) * 4 + ((key_at >> 2) & 3) - 4
    key_x = ((key_at >> 5) & 3) * 4 + (key_at & 3) - 4
    distance = jnp.maximum(jnp.abs(query_y - key_y), jnp.abs(query_x - key_x))

    @pl.loop(0, STEPS)
    def _(step):
        near = distance <= radius_ref[step // 2]
        at_y = row * 16 + (step % 2) * 8 + key_y
        for strip in (0, 1):
            at_x = col * 16 + strip * 8 + key_x
            inside = (at_y >= 0) & (at_y < grid * 16) & (at_x >= 0) & (at_x < grid * 16)
            bias[step, strip] = jnp.where(near & inside, jnp.float32(0.0), jnp.float32(LOW))

    for number, (dy, dx) in enumerate(sides):
        @pl.when(on_grid(-dy, -dx))
        def _():
            halo(number).wait_recv()

    lane = lax.broadcasted_iota(jnp.int32, (128, 128), 1)

    def unit(queries, step, strip):
        t, band = step // 2, step % 2
        k = kv[0, t, pl.ds(2 * band, 4), 2 * strip : 2 * strip + 4].reshape(512, 128)
        v = kv[1, t, pl.ds(2 * band, 4), 2 * strip : 2 * strip + 4].reshape(512, 128)
        slots = queries.shape[0] // 128
        s = lax.dot_general(queries, k, (((1,), (1,)), ((), ())), preferred_element_type=jnp.float32)
        s = s * scale
        allow = bias[step, strip]
        s = s + (allow if slots == 1 else jnp.concatenate([allow] * slots, axis=0))
        m = jnp.max(s, axis=1, keepdims=True)
        p = jnp.exp2(s - m).astype(jnp.bfloat16)
        wide = jnp.concatenate([v, jnp.ones((512, 128), jnp.bfloat16)], axis=1)
        o = jnp.dot(p, wide, preferred_element_type=jnp.float32)
        return o[:, :128], m, o[:, 128:]

    def put(ref, strips):
        for strip, (acc, m, l) in enumerate(strips):
            ref[pl.ds(strip * 128, 128), :] = acc.astype(jnp.bfloat16)
        (_, m0, l0), (_, m1, l1) = strips
        z = jnp.where(lane == 0, m0, jnp.where(lane == 1, l0, jnp.where(lane == 2, m1, jnp.where(lane == 3, l1, 0.0))))
        z = jnp.transpose(z)[:8]
        high = z.astype(jnp.bfloat16).astype(jnp.float32)
        rest = z - high
        mid = rest.astype(jnp.bfloat16).astype(jnp.float32)
        low = rest - mid
        ref[pl.ds(256, 16), :] = jnp.concatenate([high + pltpu.roll(mid, 4, 0), low], axis=0).astype(jnp.bfloat16)

    def get(ref):
        x = ref[pl.ds(256, 16), :].astype(jnp.float32)
        y = x[:8] + pltpu.roll(x[:8], 4, 0) + x[8:]
        y = jnp.transpose(jnp.concatenate([y] * 16, axis=0))
        return [(y[:, 2 * strip : 2 * strip + 1], y[:, 2 * strip + 1 : 2 * strip + 2]) for strip in (0, 1)]

    def merged(refs):
        sides_of = [get(ref) for ref in refs]
        result = []
        for strip in (0, 1):
            m = sides_of[0][strip][0]
            for one in sides_of[1:]:
                m = jnp.maximum(m, one[strip][0])
            acc, l = 0.0, 0.0
            for ref, one in zip(refs, sides_of):
                w = jnp.exp2(one[strip][0] - m)
                acc = acc + w * ref[pl.ds(strip * 128, 128), :].astype(jnp.float32)
                l = l + w * one[strip][1]
            result.append((acc, m, l))
        return result

    def masked(m, d, step, slot):
        visible = mask_ref[step // 2, 2 * (chip + d) + slot, tm]
        return jnp.where(visible > 0, m, jnp.float32(LOW))

    def alone(slot, step):
        strips = []
        for strip in (0, 1):
            acc, m, l = unit(qb[0, slot, step, strip], step, strip)
            strips.append((acc, masked(m, 0, step, slot), l))
        put(pb.at[0, slot, step], strips)

    def both(d, step):
        slots = ([], [])
        for strip in (0, 1):
            queries = qb[d, :, step, strip].reshape(256, 128)
            acc, m, l = unit(queries, step, strip)
            for slot in (0, 1):
                part = slice(128 * slot, 128 * slot + 128)
                slots[slot].append((acc[part], masked(m[part], d, step, slot), l[part]))
        for slot in (0, 1):
            put(pb.at[d, slot, step], slots[slot])

    def work(d, step):
        pair_of(d, step, other).wait_recv()
        both(d, step)
        part_of(d, step).start()

    def send_up(d, step):
        part_of(d, step).wait_recv()
        refs = [pb.at[d, core, step], rb.at[d, step]]
        if d == 1:
            @pl.when(chip >= 1)
            def _():
                up(2, step).wait_recv()

            refs.append(gb.at[0, step])
        put(ub.at[d - 1, step], merged(refs))
        up(d, step).start()

    def finish(step):
        @pl.when(core == 1)
        def _():
            part_of(0, step).wait_recv()

        @pl.when(chip >= 1)
        def _():
            up(1, step).wait_recv()

        @pl.when(chip == chips - 1)
        def _():
            up(3, step).wait_recv()

        strips = merged([pb.at[0, core, step], rb.at[0, step], gb.at[1, step], gb.at[2, step]])
        for strip, (acc, m, l) in enumerate(strips):
            attn = (acc / l).astype(jnp.bfloat16)
            for frame in (0, 1):
                ab[step, frame, strip] = attn[64 * frame : 64 * frame + 64]
        for frame in (0, 1):
            mine = head == frame * 2 + step % 2

            @pl.when(mine)
            def _():
                ar[head, step // 2] = ab[step, frame]

            @pl.when(jnp.logical_not(mine))
            def _():
                swap(step, frame).start()

    @pl.loop(0, STEPS)
    def _(step):
        alone(core, step)

        @pl.when(core == 0)
        def _():
            pair_of(0, step, other).wait_recv()
            alone(other, step)
            part_of(0, step).start()

    @pl.loop(0, STEPS + LAG_END)
    def _(i):
        @pl.when(i < STEPS)
        def _():
            @pl.when(chip < chips - 1)
            def _():
                down(0, i).wait_recv()

                @pl.when(chip >= 1)
                def _():
                    down(1, i).start()

                pair_of(1, i, core).start()

            @pl.when(chip == 0)
            def _():
                down(2, i).wait_recv()
                pair_of(3, i, core).start()

            @pl.when(chip < chips - 1)
            def _():
                work(1, i)

            @pl.when(chip == 0)
            def _():
                work(3, i)
                send_up(3, i)

            @pl.when(chip < chips - 2)
            def _():
                down(1, i).wait_recv()
                pair_of(2, i, core).start()
                work(2, i)
                send_up(2, i)

        @pl.when((i >= LAG_UP) & (i < STEPS + LAG_UP) & (chip < chips - 1))
        def _():
            send_up(1, i - LAG_UP)

        @pl.when(i >= LAG_END)
        def _():
            finish(i - LAG_END)

    for number, (dy, dx) in enumerate(sides):
        @pl.when(on_grid(dy, dx))
        def _():
            halo(number).wait_send()

    @pl.loop(0, STEPS)
    def _(step):
        @pl.when(chip >= 1)
        def _():
            down(0, step).wait_send()

        @pl.when((chip >= 1) & (chip < chips - 1))
        def _():
            down(1, step).wait_send()

        @pl.when(chip == chips - 1)
        def _():
            down(2, step).wait_send()

        @pl.when(core == 1)
        def _():
            pair_of(0, step, core).wait_send()

        @pl.when(core == 0)
        def _():
            part_of(0, step).wait_send()

        for d, there in ((1, chip < chips - 1), (2, chip < chips - 2), (3, chip == 0)):
            @pl.when(there)
            def _():
                pair_of(d, step, core).wait_send()
                part_of(d, step).wait_send()
                up(d, step).wait_send()

        for frame in (0, 1):
            @pl.when(head != frame * 2 + step % 2)
            def _():
                swap(step, frame).wait_send()

    for source in range(n_head):
        @pl.when(head != source)
        def _():
            for t in range(3):
                remote(
                    ab.at[0, 0], ar.at[source, t], swap_s.at[0, 0], swap_r.at[source, t],
                    {"head": (head + 1) % n_head},
                ).wait_recv()

    out_ref[...] = ar[...]


def project(a_ref, w_ref, o_ref):
    rows = jnp.concatenate([a_ref[z, t].reshape(128, 128) for z in range(4) for t in range(3)], axis=1)
    sums = jnp.dot(rows, w_ref[...], preferred_element_type=jnp.float32)
    pieces = []
    for y in range(8):
        for strip in (0, 1):
            pieces.append(sums[64 * strip + 8 * y : 64 * strip + 8 * y + 8])
    o_ref[...] = jnp.concatenate(pieces, axis=0).astype(jnp.bfloat16)


def per_device(query, keys, values, out_weight, radius, block_mask):
    width = out_weight.shape[1]
    scale = math.log2(math.e) / math.sqrt(128)
    weight = lax.all_gather(out_weight, "head", axis=0, tiled=True)
    vmem = pl.BlockSpec(memory_space=pltpu.VMEM)
    smem = pl.BlockSpec(memory_space=pltpu.SMEM)
    bf16 = jnp.bfloat16
    dma = pltpu.SemaphoreType.DMA
    attn = pl.pallas_call(
        functools.partial(attend, scale),
        out_shape=jax.ShapeDtypeStruct((4, 3, 2, 64, 128), bf16),
        in_specs=[vmem, vmem, vmem, smem, smem],
        out_specs=vmem,
        scratch_shapes=[
            pltpu.VMEM((2, 3, 6, 6, 32, 128), bf16),
            pltpu.VMEM((4, 2, STEPS, 2, 128, 128), bf16),
            pltpu.VMEM((4, 2, STEPS, ROWS, 128), bf16),
            pltpu.VMEM((4, STEPS, ROWS, 128), bf16),
            pltpu.VMEM((3, STEPS, ROWS, 128), bf16),
            pltpu.VMEM((3, STEPS, ROWS, 128), bf16),
            pltpu.VMEM((STEPS, 2, 2, 64, 128), bf16),
            pltpu.VMEM((4, 3, 2, 64, 128), bf16),
            pltpu.VMEM((STEPS, 2, 128, 512), jnp.float32),
            dma((8,)), dma((8,)),
            dma((3, STEPS)), dma((3, STEPS)),
            dma((4, STEPS)), dma((4, STEPS)),
            dma((4, STEPS)), dma((4, STEPS)),
            dma((3, STEPS)), dma((3, STEPS)),
            dma((STEPS, 2)), dma((4, 3)),
        ],
        compiler_params=pltpu.CompilerParams(
            collective_id=0, has_side_effects=True, vmem_limit_bytes=48 * 1024 * 1024
        ),
        cost_estimate=pl.CostEstimate(flops=6_400_000_000, bytes_accessed=2_000_000, transcendentals=6_000_000),
        name="attend",
    )(query.reshape(512, 384), keys.reshape(512, 384), values.reshape(512, 384), radius, block_mask)
    columns = 512
    mixed = pl.pallas_call(
        project,
        grid=(width // columns,),
        out_shape=jax.ShapeDtypeStruct((128, width), bf16),
        in_specs=[
            pl.BlockSpec((4, 3, 2, 64, 128), lambda i: (0, 0, 0, 0, 0)),
            pl.BlockSpec((1536, columns), lambda i: (0, i)),
        ],
        out_specs=pl.BlockSpec((128, columns), lambda i: (0, i)),
        compiler_params=pltpu.CompilerParams(vmem_limit_bytes=32 * 1024 * 1024),
        name="project",
    )(attn, weight)
    return mixed.reshape(1, 1, 128, width)


def solution(mesh):
    in_specs = (
        P("tm", "tile", None, None, None, "head"),
        P("tm", "tile", None, None, None, "head"),
        P("tm", "tile", None, None, None, "head"),
        P("head", None),
        P("head"),
        P("head", None, None),
    )
    out_specs = P("tm", "tile", "head", None)
    return jax.shard_map(per_device, mesh=mesh, in_specs=in_specs, out_specs=out_specs, check_vma=False)
```

time: 520 us -> 206 us (0.40)
  the two profiles are of different devices: /device:TPU:1 before, /device:TPU:290 now
where the time goes in v1:
time: 206 us; the launch traced here: 205 us
  Pallas kernels  184 us (89%)
  between operations  13.4 us (7%)
  local copies, waits for them, and re-layouts  6.67 us (3%)
    pallas_call x1, Pallas kernels, per_device(): pl.pallas_call(functools.partial(attend, scale), out_shape=jax.ShapeDtype...  182 us
    unnamed x12, local copies, waits for them, and re-layouts  6.67 us
  transfers between devices with their start and end apart: 1, of which 0 were waited for; matrix products, arithmetic and copies ran while one was open for 0% of the time, Pallas kernels for 89%

profile of v1, /device:TPU:290, one launch (start us, length us, event | category | flops | bytes accessed | tf_op | source)
XLA Modules:
  0.0 205.3 jit_solution(13109993622497013207)
XLA Ops:
  6.5 0.0 all-gather.2.cloned.1.call-start
  6.5 0.7 all-gather.2.cloned.1.call-update
  7.3 0.0 copy-start.1
  7.3 1.0 copy-done.1
  8.3 0.0 copy-start.2
  8.3 1.0 copy-done.2
  9.2 0.0 copy-start.3
  9.3 1.0 copy-done.3
  10.2 0.0 copy-start.4
  10.2 0.7 copy-done.4
  11.0 0.0 copy-start.5
  11.0 0.7 copy-done.5
  11.6 182.1 %attend.1.a_ref = bf16[4,3,2,64,128]{4,3,2,1,0:T(8,128)(2,1)S(1)} custom-call(bf16[512,384]{1,0:T(8,128)(2,1)S(1)} %bitcast.4, bf16[512,384]{1,0:T(8,128)(2,1)S(1)} %bitcast.5, bf16[512,384]{1,0:T(8,128)(2,1)S(1)} %bitcast.6, s32[3]{0:T(128)S(1)} %copy-done.5, s32[3,8,8]{2,1,0:T(8,128)S(1)} %copy-done.4), custom_call_target="tpu_custom_call" | custom-call | flops 6400000000 | bytes 2000000 | tf_op jit(solution)/shard_map/attend/pallas_call | solution.py:432
  193.8 0.0 all-gather.2.cloned.1.call-done.w_ref
  193.8 0.0 copy-start
  193.8 2.3 %copy-done = bf16[1536,1536]{1,0:T(8,128)(2,1)S(1)} copy-done((bf16[1536,1536]{1,0:T(8,128)(2,1)S(1)}, bf16[1536,1536]{1,0:T(8,128)(2,1)}, u32[]{:S(2)}) %copy-start) | copy-done | bytes 4718616
  196.1 2.3 %project.1 = bf16[128,1536]{1,0:T(8,128)(2,1)} custom-call(bf16[4,3,2,64,128]{4,3,2,1,0:T(8,128)(2,1)S(1)} %attend.1.a_ref, bf16[1536,1536]{1,0:T(8,128)(2,1)S(1)} %copy-done), custom_call_target="tpu_custom_call" | custom-call | tf_op jit(solution)/shard_map/project/pallas_call | solution.py:461
Async XLA Ops:
  6.5 187.2 %all-gather.2.cloned.1.call-start = ((), (), s32[]{:S(2)}) async-start(), calls=%async_computation | async-start | bytes 5898240 | tf_op jit(solution)/shard_map/all_gather | solution.py:427
  7.3 1.0 copy-start.1
  8.3 1.0 copy-start.2
  9.2 1.0 copy-start.3
  10.2 0.7 copy-start.4
  11.0 0.7 copy-start.5
  193.8 2.3 %copy-start = (bf16[1536,1536]{1,0:T(8,128)(2,1)S(1)}, bf16[1536,1536]{1,0:T(8,128)(2,1)}, u32[]{:S(2)}) copy-start(bf16[1536,1536]{1,0:T(8,128)(2,1)} %all-gather.2.cloned.1.call-done.w_ref) | copy-start | bytes 14155780
Sparse Core Ops, SparseCore 0:
  9.5 150.5 all-gather.1

commit v2 on v1

v2 whole, which is shorter than its diff:
```python
import functools
import math

import jax
import jax.numpy as jnp
from jax import lax
from jax.experimental import pallas as pl
from jax.experimental.pallas import tpu as pltpu
from jax.sharding import PartitionSpec as P

MESH = pl.DeviceIdType.MESH
LOW = -1e30
STEPS = 12
ROWS = 144
AHEAD = 2
LAG_END = 3


def attend(scale, q_in, k_in, v_in, w_in, radius_in, mask_in, out_ref, *scratch):
    (q_ref, k_ref, v_ref, radius_ref, mask_ref, kv, qb, pb, rb, ub, gb, ab, ar, bias, wf, total, load_s,
     halo_s, halo_r, down_s, down_r, pair_s, pair_r, part_s, part_r, up_s, up_r, swap_s, swap_r,
     weigh_s, weigh_r) = scratch
    tm = lax.axis_index("tm")
    tile = lax.axis_index("tile")
    head = lax.axis_index("head")
    n_tm = lax.axis_size("tm")
    n_head = lax.axis_size("head")
    grid = math.isqrt(lax.axis_size("tile"))
    chips = n_tm // 2
    chip, core = tm // 2, tm % 2
    other = 1 - core
    row, col = tile // grid, tile % grid
    sibling = {"tm": chip * 2 + other}

    def chip_off(d):
        return {"tm": (tm + 2 * d + n_tm) % n_tm}

    w_part = w_in.at[:, tile // 2, :, pl.ds(pl.multiple_of((2 * (tile % 2) + core) * 384, 384), 384)]
    loads = [
        pltpu.make_async_copy(src, dst, load_s.at[at])
        for at, (src, dst) in enumerate((
            (q_in, q_ref), (k_in, k_ref), (v_in, v_ref), (radius_in, radius_ref), (mask_in, mask_ref),
            (w_part, wf.at[core, tile, head]),
        ))
    ]
    for load in loads:
        load.start()

    def remote(src, dst, send, recv, device):
        return pltpu.make_async_remote_copy(
            src_ref=src, dst_ref=dst, send_sem=send, recv_sem=recv, device_id=device, device_id_type=MESH
        )

    sides = [(dy, dx) for dy in (-1, 0, 1) for dx in (-1, 0, 1) if (dy, dx) != (0, 0)]

    def on_grid(dy, dx):
        return (row + dy >= 0) & (row + dy < grid) & (col + dx >= 0) & (col + dx < grid)

    barrier = pltpu.get_barrier_semaphore()
    in_row = [{"tile": row * grid + (col + off) % grid} for off in range(1, grid)]
    in_col = [{"tile": (row + off) % grid * grid + col} for off in range(1, grid)]
    in_head = [{"head": (head + off) % n_head} for off in range(1, n_head)]
    always = [sibling] + [chip_off(d) for d in (1, 2, 3)] + in_row + in_col + in_head
    count = jnp.int32(len(always))
    for device in always:
        pl.semaphore_signal(barrier, inc=1, device_id=device, device_id_type=MESH)
    for dy, dx in sides:
        count = count + on_grid(dy, dx).astype(jnp.int32)

        @pl.when(on_grid(dy, dx))
        def _():
            pl.semaphore_signal(barrier, inc=1, device_id={"tile": tile + dy * grid + dx}, device_id_type=MESH)

    loads[0].wait()

    for frame in (0, 1):
        for band in (0, 1):
            for pair in range(4):
                rows = q_ref[pl.ds(frame * 256 + (band * 8 + pair * 2) * 16, 32), :].astype(jnp.float32)
                for strip in (0, 1):
                    both = jnp.concatenate([rows[8 * strip : 8 * strip + 8], rows[16 + 8 * strip : 24 + 8 * strip]], axis=0)
                    both = both.astype(jnp.bfloat16)
                    for t in range(3):
                        qb[0, core, 4 * t + 2 * band + strip, pl.ds(frame * 64 + pair * 16, 16), :] = both[:, 128 * t : 128 * t + 128]

    loads[1].wait()
    loads[2].wait()
    top = lax.broadcasted_iota(jnp.int32, (8, 384), 0) < 4
    for which, ref in ((0, k_ref), (1, v_ref)):
        for frame in (0, 1):
            for by in range(4):
                rows = ref[pl.ds(frame * 256 + by * 64, 64), :].astype(jnp.float32)
                for bx in range(4):
                    start = 8 * (bx // 2)
                    halves = []
                    for y in (0, 2):
                        first = rows[16 * y + start : 16 * y + start + 8]
                        second = rows[16 * y + 16 + start : 16 * y + 24 + start]
                        if bx % 2 == 0:
                            halves.append(jnp.where(top, first, pltpu.roll(second, 4, 0)))
                        else:
                            halves.append(jnp.where(top, pltpu.roll(first, 4, 0), second))
                    block = jnp.concatenate(halves, axis=0).astype(jnp.bfloat16)
                    for t in range(3):
                        kv[which, t, 1 + by, 1 + bx, pl.ds(frame * 16, 16), :] = block[:, 128 * t : 128 * t + 128]

    pl.semaphore_wait(barrier, count)

    def down(d, step):
        return remote(
            qb.at[0, core, step], qb.at[d, core, step], down_s.at[d - 1, step], down_r.at[d - 1, step], chip_off(-d)
        )

    def pair_of(d, step, slot):
        return remote(qb.at[d, slot, step], qb.at[d, slot, step], pair_s.at[d, step], pair_r.at[d, step], sibling)

    def part_of(d, step):
        return remote(pb.at[d, other, step], rb.at[d, step], part_s.at[d, step], part_r.at[d, step], sibling)

    def up(d, step):
        return remote(ub.at[d - 1, step], gb.at[d - 1, step], up_s.at[d - 1, step], up_r.at[d - 1, step], chip_off(d))

    def weigh(stage, at):
        mine = (
            wf.at[core, tile, head], wf.at[core, tile], wf.at[core, pl.ds(row * grid, grid)], wf.at[core],
        )[stage]
        to = (in_head, in_row, in_col, [sibling])[stage][at]
        return remote(mine, mine, weigh_s.at[stage, at], weigh_r.at[stage, at], to)

    def weigh_got(stage, at):
        off = at + 1
        there = (
            wf.at[core, tile, (head + n_head - off) % n_head],
            wf.at[core, row * grid + (col + grid - off) % grid],
            wf.at[core, pl.ds((row + grid - off) % grid * grid, grid)],
            wf.at[other],
        )[stage]
        to = (in_head, in_row, in_col, [sibling])[stage][at]
        return remote(there, there, weigh_s.at[stage, at], weigh_r.at[stage, at], to)

    stage_sizes = (n_head - 1, grid - 1, grid - 1, 1)

    def halo(number):
        dy, dx = sides[number]
        src = {-1: slice(1, 2), 0: slice(1, 5), 1: slice(4, 5)}
        dst = {-1: slice(5, 6), 0: slice(1, 5), 1: slice(0, 1)}
        return remote(
            kv.at[:, :, src[dy], src[dx]], kv.at[:, :, dst[dy], dst[dx]], halo_s.at[number], halo_r.at[number],
            {"tile": (tile + dy * grid + dx) % (grid * grid)},
        )

    def swap(step, frame):
        return remote(
            ab.at[step, frame], ar.at[head, step // 4, step % 2],
            swap_s.at[step, frame], swap_r.at[head, step // 4, step % 2], {"head": frame * 2 + step // 2 % 2},
        )

    def send_queries(step):
        for d in (1, 2, 3):
            @pl.when(chip >= d)
            def _():
                down(d, step).start()

    @pl.loop(0, AHEAD)
    def _(step):
        send_queries(step)

    @pl.when(core == 1)
    def _():
        @pl.loop(0, STEPS)
        def _(step):
            pair_of(0, step, core).start()

    for number, (dy, dx) in enumerate(sides):
        @pl.when(on_grid(dy, dx))
        def _():
            halo(number).start()

    loads[5].wait()
    for at in range(stage_sizes[0]):
        weigh(0, at).start()

    none = jnp.zeros((2, 3, 1, 6, 32, 128), jnp.bfloat16)
    for edge, at in ((row == 0, 0), (row == grid - 1, 5)):
        @pl.when(edge)
        def _():
            kv[:, :, at : at + 1, :] = none
    for edge, at in ((col == 0, 0), (col == grid - 1, 5)):
        @pl.when(edge)
        def _():
            kv[:, :, :, at : at + 1] = none.reshape(2, 3, 6, 1, 32, 128)

    def without(ref):
        @pl.loop(0, STEPS)
        def _(step):
            ref[step] = jnp.concatenate([jnp.zeros((128, 128), jnp.float32), jnp.full((16, 128), LOW, jnp.float32)], axis=0).astype(jnp.bfloat16)

    for d in (1, 2, 3):
        @pl.when(chip < d)
        def _():
            without(gb.at[d - 1])

    @pl.when(core == 0)
    def _():
        without(rb.at[0])

    loads[3].wait()
    loads[4].wait()
    query_at = lax.broadcasted_iota(jnp.int32, (128, 512), 0)
    key_at = lax.broadcasted_iota(jnp.int32, (128, 512), 1)
    query_y, query_x = (query_at >> 3) & 7, query_at & 7
    key_y = ((key_at >> 7) & 3) * 4 + ((key_at >> 2) & 3) - 4
    key_x = ((key_at >> 5) & 3) * 4 + (key_at & 3) - 4
    distance = jnp.maximum(jnp.abs(query_y - key_y), jnp.abs(query_x - key_x))

    @pl.loop(0, STEPS)
    def _(step):
        near = distance <= radius_ref[step // 4]
        at_y = row * 16 + (step // 2 % 2) * 8 + key_y
        at_x = col * 16 + (step % 2) * 8 + key_x
        inside = (at_y >= 0) & (at_y < grid * 16) & (at_x >= 0) & (at_x < grid * 16)
        bias[step] = jnp.where(near & inside, jnp.float32(0.0), jnp.float32(LOW))

    for number, (dy, dx) in enumerate(sides):
        @pl.when(on_grid(-dy, -dx))
        def _():
            halo(number).wait_recv()

    lane = lax.broadcasted_iota(jnp.int32, (128, 128), 1)

    def unit(queries, step):
        t, band, strip = step // 4, step // 2 % 2, step % 2
        k = kv[0, t, pl.ds(2 * band, 4), pl.ds(2 * strip, 4)].reshape(512, 128)
        v = kv[1, t, pl.ds(2 * band, 4), pl.ds(2 * strip, 4)].reshape(512, 128)
        slots = queries.shape[0] // 128
        s = lax.dot_general(queries, k, (((1,), (1,)), ((), ())), preferred_element_type=jnp.float32)
        s = s * scale
        allow = bias[step]
        s = s + (allow if slots == 1 else jnp.concatenate([allow] * slots, axis=0))
        m = jnp.max(s, axis=1, keepdims=True)
        p = jnp.exp2(s - m).astype(jnp.bfloat16)
        wide = jnp.concatenate([v, jnp.ones((512, 128), jnp.bfloat16)], axis=1)
        o = jnp.dot(p, wide, preferred_element_type=jnp.float32)
        return o[:, :128], m, o[:, 128:]

    def put(ref, acc, m, l):
        ref[pl.ds(0, 128), :] = acc.astype(jnp.bfloat16)
        z = jnp.transpose(jnp.where(lane == 0, m, jnp.where(lane == 1, l, 0.0)))[:8]
        high = z.astype(jnp.bfloat16).astype(jnp.float32)
        rest = z - high
        mid = rest.astype(jnp.bfloat16).astype(jnp.float32)
        low = rest - mid
        ref[pl.ds(128, 16), :] = jnp.concatenate([high + pltpu.roll(mid, 4, 0), low], axis=0).astype(jnp.bfloat16)

    def get(ref):
        x = ref[pl.ds(128, 16), :].astype(jnp.float32)
        y = x[:8] + pltpu.roll(x[:8], 4, 0) + x[8:]
        y = jnp.transpose(jnp.concatenate([y] * 16, axis=0))
        return y[:, 0:1], y[:, 1:2]

    def merged(refs):
        sides_of = [get(ref) for ref in refs]
        m = sides_of[0][0]
        for one in sides_of[1:]:
            m = jnp.maximum(m, one[0])
        acc, l = 0.0, 0.0
        for ref, one in zip(refs, sides_of):
            w = jnp.exp2(one[0] - m)
            acc = acc + w * ref[pl.ds(0, 128), :].astype(jnp.float32)
            l = l + w * one[1]
        return acc, m, l

    def masked(m, d, step, slot):
        visible = mask_ref[step // 4, 2 * (chip + d) + slot, tm]
        return jnp.where(visible > 0, m, jnp.float32(LOW))

    def alone(slot, step):
        acc, m, l = unit(qb[0, slot, step], step)
        put(pb.at[0, slot, step], acc, masked(m, 0, step, slot), l)

    def both(d, step):
        acc, m, l = unit(qb[d, :, step].reshape(256, 128), step)
        for slot in (0, 1):
            part = slice(128 * slot, 128 * slot + 128)
            put(pb.at[d, slot, step], acc[part], masked(m[part], d, step, slot), l[part])

    def work(d, step):
        pair_of(d, step, other).wait_recv()
        both(d, step)
        part_of(d, step).start()

    def send_up(d, step):
        part_of(d, step).wait_recv()
        put(ub.at[d - 1, step], *merged([pb.at[d, core, step], rb.at[d, step]]))
        up(d, step).start()

    def finish(step):
        @pl.when(core == 1)
        def _():
            part_of(0, step).wait_recv()

        for d in (1, 2, 3):
            @pl.when(chip >= d)
            def _():
                up(d, step).wait_recv()

        acc, _, l = merged([pb.at[0, core, step], rb.at[0, step]] + [gb.at[d - 1, step] for d in (1, 2, 3)])
        attn = (acc / l).astype(jnp.bfloat16)
        for frame in (0, 1):
            ab[step, frame] = attn[64 * frame : 64 * frame + 64]
        for frame in (0, 1):
            mine = head == frame * 2 + step // 2 % 2

            @pl.when(mine)
            def _():
                ar[head, step // 4, step % 2] = ab[step, frame]

            @pl.when(jnp.logical_not(mine))
            def _():
                swap(step, frame).start()

    @pl.loop(0, STEPS + LAG_END)
    def _(i):
        @pl.when(i < STEPS)
        def _():
            for d in (1, 2, 3):
                @pl.when(chip >= d)
                def _():
                    down(d, i).wait_send()

            @pl.when(i + AHEAD < STEPS)
            def _():
                send_queries(i + AHEAD)

            for d in (1, 2, 3):
                @pl.when(chip + d < chips)
                def _():
                    down(d, i).wait_recv()
                    pair_of(d, i, core).start()

            for d in (1, 2, 3):
                @pl.when(chip + d < chips)
                def _():
                    work(d, i)

            alone(core, i)

            @pl.when(core == 0)
            def _():
                pair_of(0, i, other).wait_recv()
                alone(other, i)
                part_of(0, i).start()

            for d in (1, 2, 3):
                @pl.when(chip + d < chips)
                def _():
                    send_up(d, i)

        for stage, when in ((0, 1), (1, 4), (2, 9)):
            @pl.when(i == when)
            def _():
                for at in range(stage_sizes[stage]):
                    weigh_got(stage, at).wait_recv()
                for at in range(stage_sizes[stage + 1]):
                    weigh(stage + 1, at).start()

        @pl.when(i >= LAG_END)
        def _():
            finish(i - LAG_END)

    weigh_got(3, 0).wait_recv()

    for t in range(3):
        for source in range(n_head):
            @pl.when(head != source)
            def _():
                for strip in (0, 1):
                    remote(
                        ab.at[0, 0], ar.at[source, t, strip], swap_s.at[0, 0], swap_r.at[source, t, strip],
                        {"head": (head + 1) % n_head},
                    ).wait_recv()

        rows = jnp.concatenate([ar[z, t].reshape(128, 128) for z in range(4)], axis=1)
        for part in range(4):
            at = slice(384 * part, 384 * part + 384)
            weight = jnp.concatenate(
                [wf[part % 2, 2 * group + part // 2, z, t] for z in range(4) for group in range(8)], axis=0
            )
            sums = jnp.dot(rows, weight, preferred_element_type=jnp.float32)
            if t > 0:
                sums = sums + total[:, at]
            if t < 2:
                total[:, at] = sums
            else:
                pieces = [
                    sums[64 * strip + 8 * y : 64 * strip + 8 * y + 8] for y in range(8) for strip in (0, 1)
                ]
                out_ref[:, at] = jnp.concatenate(pieces, axis=0).astype(jnp.bfloat16)

    for number, (dy, dx) in enumerate(sides):
        @pl.when(on_grid(dy, dx))
        def _():
            halo(number).wait_send()

    @pl.loop(0, STEPS)
    def _(step):
        @pl.when(core == 1)
        def _():
            pair_of(0, step, core).wait_send()

        @pl.when(core == 0)
        def _():
            part_of(0, step).wait_send()

        for d in (1, 2, 3):
            @pl.when(chip + d < chips)
            def _():
                pair_of(d, step, core).wait_send()
                part_of(d, step).wait_send()
                up(d, step).wait_send()

        for frame in (0, 1):
            @pl.when(head != frame * 2 + step // 2 % 2)
            def _():
                swap(step, frame).wait_send()

    for stage, size in enumerate(stage_sizes):
        for at in range(size):
            weigh(stage, at).wait_send()


def per_device(query, keys, values, out_weight, radius, block_mask):
    width = out_weight.shape[1]
    scale = math.log2(math.e) / math.sqrt(128)
    bf16 = jnp.bfloat16
    dma = pltpu.SemaphoreType.DMA
    mixed = pl.pallas_call(
        functools.partial(attend, scale),
        out_shape=jax.ShapeDtypeStruct((128, width), bf16),
        in_specs=[pl.BlockSpec(memory_space=pl.ANY)] * 6,
        out_specs=pl.BlockSpec(memory_space=pltpu.VMEM),
        scratch_shapes=[
            pltpu.VMEM((512, 384), bf16),
            pltpu.VMEM((512, 384), bf16),
            pltpu.VMEM((512, 384), bf16),
            pltpu.SMEM((3,), jnp.int32),
            pltpu.SMEM((3, 8, 8), jnp.int32),
            pltpu.VMEM((2, 3, 6, 6, 32, 128), bf16),
            pltpu.VMEM((4, 2, STEPS, 128, 128), bf16),
            pltpu.VMEM((4, 2, STEPS, ROWS, 128), bf16),
            pltpu.VMEM((4, STEPS, ROWS, 128), bf16),
            pltpu.VMEM((3, STEPS, ROWS, 128), bf16),
            pltpu.VMEM((3, STEPS, ROWS, 128), bf16),
            pltpu.VMEM((STEPS, 2, 64, 128), bf16),
            pltpu.VMEM((4, 3, 2, 64, 128), bf16),
            pltpu.VMEM((STEPS, 128, 512), jnp.float32),
            pltpu.VMEM((2, 16, 4, 3, 16, 384), bf16),
            pltpu.VMEM((128, width), jnp.float32),
            dma((6,)),
            dma((8,)), dma((8,)),
            dma((3, STEPS)), dma((3, STEPS)),
            dma((4, STEPS)), dma((4, STEPS)),
            dma((4, STEPS)), dma((4, STEPS)),
            dma((3, STEPS)), dma((3, STEPS)),
            dma((STEPS, 2)), dma((4, 3, 2)),
            dma((4, 3)), dma((4, 3)),
        ],
        compiler_params=pltpu.CompilerParams(
            collective_id=0, has_side_effects=True, vmem_limit_bytes=60 * 1024 * 1024
        ),
        cost_estimate=pl.CostEstimate(flops=6_400_000_000, bytes_accessed=2_000_000, transcendentals=6_000_000),
        name="attend",
    )(
        query.reshape(512, 384), keys.reshape(512, 384), values.reshape(512, 384),
        out_weight.reshape(3, 8, 16, width), radius, block_mask,
    )
    return mixed.reshape(1, 1, 128, width)


def solution(mesh):
    in_specs = (
        P("tm", "tile", None, None, None, "head"),
        P("tm", "tile", None, None, None, "head"),
        P("tm", "tile", None, None, None, "head"),
        P("head", None),
        P("head"),
        P("head", None, None),
    )
    out_specs = P("tm", "tile", "head", None)
    return jax.shard_map(per_device, mesh=mesh, in_specs=in_specs, out_specs=out_specs, check_vma=False)
```

time: 206 us -> 123 us (0.60)
  the two profiles are of different devices: /device:TPU:290 before, /device:TPU:1 now
where the time goes in v2:
time: 123 us; the launch traced here: 121 us
  Pallas kernels  119 us (97%)
  local copies, waits for them, and re-layouts  1.77 us (1%)
    pallas_call x1, Pallas kernels, per_device(): pl.pallas_call(functools.partial(attend, scale), out_shape=jax.ShapeDtype...  119 us

profile of v2, /device:TPU:1, one launch (start us, length us, event | category | flops | bytes accessed | tf_op | source)
XLA Modules:
  0.0 121.2 jit_solution(805700309823985438)
XLA Ops:
  0.0 119.4 %attend.1 = bf16[128,1536]{1,0:T(8,128)(2,1)} custom-call(bf16[512,384]{1,0:T(8,128)(2,1)} %bitcast.7, bf16[512,384]{1,0:T(8,128)(2,1)} %bitcast.8, bf16[512,384]{1,0:T(8,128)(2,1)} %bitcast.9, bf16[3,8,16,1536]{3,2,1,0:T(8,128)(2,1)} %bitcast.6, s32[3]{0:T(128)} %radius_in.1, s32[3,8,8]{2,1,0:T(8,128)} %mask_in.1), custom_call_target="tpu_custom_call" | custom-call | flops 6400000000 | bytes 2000000 | tf_op jit(solution)/shard_map/attend/pallas_call | solution.py:437
  119.4 1.8 %copy.8 = bf16[1,1,128,1536]{3,2,1,0:T(8,128)(2,1)} copy(bf16[1,1,128,1536]{3,2,1,0:T(8,128)(2,1)} %bitcast.5) | data formatting | bytes 786432

commit v3 on v2

--- a/solution.py
+++ b/solution.py
@@ -13,7 +13,7 @@
 STEPS = 12
 ROWS = 144
 AHEAD = 2
-LAG_END = 3
+LAG_END = 2
 
 
 def attend(scale, q_in, k_in, v_in, w_in, radius_in, mask_in, out_ref, *scratch):
@@ -161,6 +161,11 @@
             def _():
                 down(d, step).start()
 
+    for number, (dy, dx) in enumerate(sides):
+        @pl.when(on_grid(dy, dx))
+        def _():
+            halo(number).start()
+
     @pl.loop(0, AHEAD)
     def _(step):
         send_queries(step)
@@ -170,11 +175,6 @@
         @pl.loop(0, STEPS)
         def _(step):
             pair_of(0, step, core).start()
-
-    for number, (dy, dx) in enumerate(sides):
-        @pl.when(on_grid(dy, dx))
-        def _():
-            halo(number).start()
 
     loads[5].wait()
     for at in range(stage_sizes[0]):
@@ -243,23 +243,28 @@
         o = jnp.dot(p, wide, preferred_element_type=jnp.float32)
         return o[:, :128], m, o[:, 128:]
 
-    def put(ref, acc, m, l):
-        ref[pl.ds(0, 128), :] = acc.astype(jnp.bfloat16)
-        z = jnp.transpose(jnp.where(lane == 0, m, jnp.where(lane == 1, l, 0.0)))[:8]
-        high = z.astype(jnp.bfloat16).astype(jnp.float32)
-        rest = z - high
-        mid = rest.astype(jnp.bfloat16).astype(jnp.float32)
-        low = rest - mid
-        ref[pl.ds(128, 16), :] = jnp.concatenate([high + pltpu.roll(mid, 4, 0), low], axis=0).astype(jnp.bfloat16)
-
-    def get(ref):
-        x = ref[pl.ds(128, 16), :].astype(jnp.float32)
-        y = x[:8] + pltpu.roll(x[:8], 4, 0) + x[8:]
-        y = jnp.transpose(jnp.concatenate([y] * 16, axis=0))
-        return y[:, 0:1], y[:, 1:2]
+    def put(entries):
+        z = jnp.zeros((128, 128), jnp.float32)
+        for at, (ref, acc, m, l) in enumerate(entries):
+            ref[pl.ds(0, 128), :] = acc.astype(jnp.bfloat16)
+            z = jnp.where(lane == 8 * at, m, jnp.where(lane == 8 * at + 1, l, z))
+        z = jnp.transpose(z)
+        for at, (ref, _, _, _) in enumerate(entries):
+            own = z[8 * at : 8 * at + 8]
+            high = own.astype(jnp.bfloat16).astype(jnp.float32)
+            rest = own - high
+            mid = rest.astype(jnp.bfloat16).astype(jnp.float32)
+            low = rest - mid
+            ref[pl.ds(128, 16), :] = jnp.concatenate([high + pltpu.roll(mid, 4, 0), low], axis=0).astype(jnp.bfloat16)
 
     def merged(refs):
-        sides_of = [get(ref) for ref in refs]
+        packed = []
+        for ref in refs:
+            x = ref[pl.ds(128, 16), :].astype(jnp.float32)
+            packed.append(x[:8] + pltpu.roll(x[:8], 4, 0) + x[8:])
+        packed = jnp.concatenate(packed + [packed[0]] * (16 - len(refs)), axis=0)
+        columns = jnp.transpose(packed)
+        sides_of = [(columns[:, 8 * at : 8 * at + 1], columns[:, 8 * at + 1 : 8 * at + 2]) for at in range(len(refs))]
         m = sides_of[0][0]
         for one in sides_of[1:]:
             m = jnp.maximum(m, one[0])
@@ -276,13 +281,15 @@
 
     def alone(slot, step):
         acc, m, l = unit(qb[0, slot, step], step)
-        put(pb.at[0, slot, step], acc, masked(m, 0, step, slot), l)
+        put([(pb.at[0, slot, step], acc, masked(m, 0, step, slot), l)])
 
     def both(d, step):
         acc, m, l = unit(qb[d, :, step].reshape(256, 128), step)
+        entries = []
         for slot in (0, 1):
             part = slice(128 * slot, 128 * slot + 128)
-            put(pb.at[d, slot, step], acc[part], masked(m[part], d, step, slot), l[part])
+            entries.append((pb.at[d, slot, step], acc[part], masked(m[part], d, step, slot), l[part]))
+        put(entries)
 
     def work(d, step):
         pair_of(d, step, other).wait_recv()
@@ -291,7 +298,7 @@
 
     def send_up(d, step):
         part_of(d, step).wait_recv()
-        put(ub.at[d - 1, step], *merged([pb.at[d, core, step], rb.at[d, step]]))
+        put([(ub.at[d - 1, step], *merged([pb.at[d, core, step], rb.at[d, step]]))])
         up(d, step).start()
 
     def finish(step):
@@ -328,27 +335,29 @@
                 def _():
                     down(d, i).wait_send()
 
-            @pl.when(i + AHEAD < STEPS)
-            def _():
-                send_queries(i + AHEAD)
-
             for d in (1, 2, 3):
                 @pl.when(chip + d < chips)
                 def _():
                     down(d, i).wait_recv()
                     pair_of(d, i, core).start()
 
+            @pl.when(i + AHEAD < STEPS)
+            def _():
+                send_queries(i + AHEAD)
+
             for d in (1, 2, 3):
                 @pl.when(chip + d < chips)
                 def _():
                     work(d, i)
 
-            alone(core, i)
+            @pl.when(core == 1)
+            def _():
+                alone(core, i)
 
             @pl.when(core == 0)
             def _():
                 pair_of(0, i, other).wait_recv()
-                alone(other, i)
+                both(0, i)
                 part_of(0, i).start()
 
             for d in (1, 2, 3):

time: 123 us -> 123 us (level)
  no operation moved by 1% of the time
where the time goes in v3:
time: 123 us; the launch traced here: 121 us
  Pallas kernels  120 us (98%)
  local copies, waits for them, and re-layouts  1.77 us (1%)
    pallas_call x1, Pallas kernels, per_device(): pl.pallas_call(functools.partial(attend, scale), out_shape=jax.ShapeDtype...  120 us

profile of v3, /device:TPU:1, one launch (start us, length us, event | category | flops | bytes accessed | tf_op | source)
XLA Modules:
  0.0 121.4 jit_solution(15654248449473531043)
XLA Ops:
  0.0 119.7 %attend.1 = bf16[128,1536]{1,0:T(8,128)(2,1)} custom-call(bf16[512,384]{1,0:T(8,128)(2,1)} %bitcast.7, bf16[512,384]{1,0:T(8,128)(2,1)} %bitcast.8, bf16[512,384]{1,0:T(8,128)(2,1)} %bitcast.9, bf16[3,8,16,1536]{3,2,1,0:T(8,128)(2,1)} %bitcast.6, s32[3]{0:T(128)} %radius_in.1, s32[3,8,8]{2,1,0:T(8,128)} %mask_in.1), custom_call_target="tpu_custom_call" | custom-call | flops 6400000000 | bytes 2000000 | tf_op jit(solution)/shard_map/attend/pallas_call | solution.py:446
  119.7 1.8 %copy.8 = bf16[1,1,128,1536]{3,2,1,0:T(8,128)(2,1)} copy(bf16[1,1,128,1536]{3,2,1,0:T(8,128)(2,1)} %bitcast.5) | data formatting | bytes 786432

commit v4 on v3

--- a/solution.py
+++ b/solution.py
@@ -155,9 +155,17 @@
             swap_s.at[step, frame], swap_r.at[head, step // 4, step % 2], {"head": frame * 2 + step // 2 % 2},
         )
 
+    def relay(step):
+        return remote(
+            qb.at[3, core, step], qb.at[2, core, step], down_s.at[1, step], down_r.at[1, step], chip_off(1)
+        )
+
+    def sends(d):
+        return chip == d if d == 2 else chip >= d
+
     def send_queries(step):
         for d in (1, 2, 3):
-            @pl.when(chip >= d)
+            @pl.when(sends(d))
             def _():
                 down(d, step).start()
 
@@ -331,19 +339,21 @@
         @pl.when(i < STEPS)
         def _():
             for d in (1, 2, 3):
-                @pl.when(chip >= d)
+                @pl.when(sends(d))
                 def _():
                     down(d, i).wait_send()
 
-            for d in (1, 2, 3):
+            @pl.when(i + AHEAD < STEPS)
+            def _():
+                send_queries(i + AHEAD)
+
+            for d in (3, 1, 2):
                 @pl.when(chip + d < chips)
                 def _():
                     down(d, i).wait_recv()
+                    if d == 3:
+                        relay(i).start()
                     pair_of(d, i, core).start()
-
-            @pl.when(i + AHEAD < STEPS)
-            def _():
-                send_queries(i + AHEAD)
 
             for d in (1, 2, 3):
                 @pl.when(chip + d < chips)
@@ -427,6 +437,8 @@
                 pair_of(d, step, core).wait_send()
                 part_of(d, step).wait_send()
                 up(d, step).wait_send()
+                if d == 3:
+                    relay(step).wait_send()
 
         for frame in (0, 1):
             @pl.when(head != frame * 2 + step // 2 % 2)

time: 123 us -> 145 us (1.18)
  the two profiles are of different devices: /device:TPU:1 before, /device:TPU:508 now
where the time goes in v4:
time: 145 us; the launch traced here: 144 us
  Pallas kernels  143 us (99%)
  local copies, waits for them, and re-layouts  1.77 us (1%)
    pallas_call x1, Pallas kernels, per_device(): pl.pallas_call(functools.partial(attend, scale), out_shape=jax.ShapeDtype...  143 us

profile of v4, /device:TPU:508, one launch (start us, length us, event | category | flops | bytes accessed | tf_op | source)
XLA Modules:
  0.0 144.4 jit_solution(7036037823160644315)
XLA Ops:
  0.0 142.6 %attend.1 = bf16[128,1536]{1,0:T(8,128)(2,1)} custom-call(bf16[512,384]{1,0:T(8,128)(2,1)} %bitcast.7, bf16[512,384]{1,0:T(8,128)(2,1)} %bitcast.8, bf16[512,384]{1,0:T(8,128)(2,1)} %bitcast.9, bf16[3,8,16,1536]{3,2,1,0:T(8,128)(2,1)} %bitcast.6, s32[3]{0:T(128)} %radius_in.1, s32[3,8,8]{2,1,0:T(8,128)} %mask_in.1), custom_call_target="tpu_custom_call" | custom-call | flops 6400000000 | bytes 2000000 | tf_op jit(solution)/shard_map/attend/pallas_call | solution.py:458
  142.7 1.8 %copy.8 = bf16[1,1,128,1536]{3,2,1,0:T(8,128)(2,1)} copy(bf16[1,1,128,1536]{3,2,1,0:T(8,128)(2,1)} %bitcast.5) | data formatting | bytes 786432
